TPU v7x, 32 devices: a whole 2x2x4 slice. The times are simulated.
32 devices in a mesh: row: 4 (over z), col: 8 (over y, x, core).
Axes of the slice: x: 2, y: 2, z: 4, core: 2. Of those that a mesh axis runs over, the one named last changes fastest.
Arguments:
- lower_vectors: bfloat16 [192, 65536], P('col', 'row'), may hold values from -0.0234375 to 0.0234375
- upper_vectors: bfloat16 [1024, 65536], P('col', 'row'), may hold values from -0.0234375 to 0.0234375
- vib_dipole: bfloat16 [3, 256, 256], replicated, may hold values from -96 to 96
- rot_factor: float32 [3, 256], P(None, 'row'), may hold values from 0.5 to 1.5
- population: float32 [192], P('row'), may hold values from 0.02 to 0.4
- broadening: float32 [192], P('row'), may hold values from 0.5 to 2
- lower_symmetry: int32 [192], P('row'), may hold values from 0 to 7
- upper_symmetry: int32 [1024], P('col'), may hold values from 0 to 7
- symmetry_pairs: int32 [8], replicated, may hold values from 0 to 7, each once
- width_class: int32 [192, 1024], P('row', 'col'), may hold values from 0 to 7
- width_table: float32 [8], replicated, may hold values from 0.5 to 6
- line_shard: int32 [192, 1024], P('row', 'col'), may hold values from 0 to 31, as said below
- line_bin: int32 [192, 1024], P('row', 'col'), may hold values from 0 to 8191
- bin_offset: float32 [192, 1024], P('row', 'col'), may hold values from 0 to 1
Outputs:
- amplitudes: float32 [192, 1024], P('row', 'col')
- spectrum: float32 [262144], P(('row', 'col'))
Inputs may be any that keep to these rules, and one draw needn't show every extreme that they name: `line_shard`: for each device's block of lines (48 lower by 128 upper states), exactly 768 lines name one grid shard that is common to all devices and drawn from the seed; each other shard is named by the block's lines an equal number of times up to one.
All inputs are finite; a program needn't handle non-finite values.
Results may differ from a plain program's by a relative error of at most 0.0029.
Values may be sent and summed in bfloat16 or wider, within the bound.
A program may use at most 128 MiB of HBM per device.

v0:
```python
import math

import jax
import jax.numpy as jnp
from jax import lax
from jax.sharding import PartitionSpec as P

NV = 256
HW = 64
GRID_DEV = 8192


doppler_base = 1.5
log_two = math.log(2.0)


def extended(value, sides, width):
    for axis, dim in sides:
        size, length = (lax.axis_size(axis), value.shape[dim])
        up = [(i, (i + 1) % size) for i in range(size - 1)]
        down = [(j, i) for i, j in up]
        last = lax.slice_in_dim(value, length - width, length, axis=dim)
        first = lax.slice_in_dim(value, 0, width, axis=dim)
        before = lax.ppermute(last, axis, up)
        after = lax.ppermute(first, axis, down)
        value = jnp.concatenate([before, value, after], axis=dim)
    return value


def passed_along(value, axis, by):
    size = lax.axis_size(axis)
    pairs = [(i, i + by) for i in range(size) if 0 <= i + by < size]
    return lax.ppermute(value, axis, pairs)


def apply_dipole(upper_vectors, vib_dipole, rot_factor):
    upper_count, basis_rows = upper_vectors.shape
    k_slab = upper_vectors.reshape(upper_count, basis_rows // NV, NV)
    padded = extended(k_slab, (("row", 1),), 1)
    slab_rows = k_slab.shape[1]
    summed = jnp.zeros(k_slab.shape, jnp.float32)
    for band_index in range(3):
        shifted = padded[:, band_index : band_index + slab_rows, :]
        product_band = jnp.einsum(
            "ukj,ij->uki", shifted, vib_dipole[band_index], preferred_element_type=jnp.float32
        )
        summed = summed + rot_factor[band_index][None, :, None] * product_band
    return summed.astype(jnp.bfloat16).reshape(upper_count, basis_rows)


def strengths(amplitudes, population, lower_symmetry, upper_symmetry, symmetry_pairs):
    sym_count = symmetry_pairs.shape[0]
    choose = (lower_symmetry[:, None] == jnp.arange(sym_count)[None, :]).astype(jnp.int32)
    allowed = jnp.sum(choose * symmetry_pairs[None, :], axis=1)
    keep_mask = (upper_symmetry[None, :] == allowed[:, None]).astype(jnp.float32)
    return population[:, None] * amplitudes * amplitudes * keep_mask


def lorentz_widths(width_class, width_table, broadening):
    classes = width_table.shape[0]
    class_hits = (width_class[:, :, None] == jnp.arange(classes)[None, None, :]).astype(jnp.float32)
    return jnp.sum(class_hits * width_table[None, None, :], axis=2) * broadening[:, None]


def tile_binning(values, shard_base, grid_total):
    strength = values[0]
    offset = values[1]
    lorentz = values[2]
    position = values[3].astype(jnp.int32)
    tile = min(128, GRID_DEV)
    tiles = GRID_DEV // tile
    width = tile + 2 * HW
    tile_of = position // tile
    inside = position - tile_of * tile
    columns = jnp.arange(width, dtype=jnp.int32)
    step_grid = columns[None, :] - inside[:, None] - HW
    valid = (step_grid >= -HW) & (step_grid < HW)
    distance = step_grid.astype(jnp.float32) - offset[:, None]
    square = distance * distance
    center = (shard_base + position).astype(jnp.float32) + offset
    doppler = doppler_base * (1.0 + center / grid_total)
    gauss_part = (
        math.sqrt(log_two / math.pi)
        / doppler[:, None]
        * jnp.exp(-log_two * square / (doppler * doppler)[:, None])
    )
    lorentz_part = lorentz[:, None] / (math.pi * (square + (lorentz * lorentz)[:, None]))
    mixing = lorentz / (lorentz + doppler)
    profile = mixing[:, None] * lorentz_part + (1.0 - mixing)[:, None] * gauss_part
    windows = jnp.where(valid, strength[:, None] * profile, 0.0)
    onehot = (tile_of[None, :] == jnp.arange(tiles, dtype=jnp.int32)[:, None]).astype(jnp.float32)
    summed = jnp.dot(
        onehot, windows, precision=lax.Precision.HIGHEST, preferred_element_type=jnp.float32
    )
    head = jnp.pad(summed[:, :tile].reshape(-1), (0, tile))
    tail = summed[:, tile:].reshape(-1)
    tail = jnp.pad(tail, (tile, 0))
    return head + tail


def pack_lines(strength, lorentz, line_shard, line_bin, bin_offset, devices):
    line_count = strength.size
    capacity = 4 * line_count // devices
    line_owner = line_shard.reshape(-1)
    line_order = jnp.argsort(line_owner, stable=True)
    sorted_owner = line_owner[line_order]
    line_index = jnp.arange(line_count, dtype=jnp.int32)
    boundary = jnp.concatenate([jnp.ones((1,), bool), sorted_owner[1:] != sorted_owner[:-1]])
    run_start = lax.cummax(jnp.where(boundary, line_index, 0), axis=0)
    slot_index = sorted_owner * capacity + (line_index - run_start)
    payload = jnp.stack(
        [
            strength.reshape(-1),
            bin_offset.reshape(-1),
            lorentz.reshape(-1),
            line_bin.reshape(-1).astype(jnp.float32),
        ]
    )[:, line_order]
    filler = jnp.zeros((4, devices * capacity), jnp.float32).at[2].set(1.0)
    return filler.at[:, slot_index].set(payload).reshape(4, devices, capacity)


def by_lines(strength, lorentz, line_shard, line_bin, bin_offset, devices, grid_total):
    outgoing = pack_lines(strength, lorentz, line_shard, line_bin, bin_offset, devices)
    capacity = outgoing.shape[2]
    incoming = lax.all_to_all(outgoing, ("row", "col"), split_axis=1, concat_axis=1, tiled=True)
    groups = devices // 4
    blocks = incoming.reshape(4, groups, 4 * capacity)
    grid_base = lax.axis_index(("row", "col")) * GRID_DEV

    def add_group(group_index, buffer):
        values = lax.dynamic_index_in_dim(blocks, group_index, 1, keepdims=False)
        return buffer + tile_binning(values, grid_base, grid_total)

    padded = lax.fori_loop(0, groups, add_group, jnp.zeros((GRID_DEV + 2 * HW,), jnp.float32))
    from_left = passed_along(padded[GRID_DEV + HW :], ("row", "col"), 1)
    from_right = passed_along(padded[:HW], ("row", "col"), -1)
    own_cells = padded[HW : GRID_DEV + HW]
    return own_cells.at[:HW].add(from_left).at[GRID_DEV - HW :].add(from_right)


def shards(
    lower_vectors,
    upper_vectors,
    vib_dipole,
    rot_factor,
    population,
    broadening,
    lower_symmetry,
    upper_symmetry,
    symmetry_pairs,
    width_class,
    width_table,
    line_shard,
    line_bin,
    bin_offset,
):
    weighted = apply_dipole(upper_vectors, vib_dipole, rot_factor)
    partial_value = lax.dot_general(
        lax.all_gather(lower_vectors, "col", axis=0, tiled=True),
        weighted,
        (((1,), (1,)), ((), ())),
        preferred_element_type=jnp.float32,
    )
    amplitudes = lax.psum_scatter(partial_value, "row", scatter_dimension=0, tiled=True)
    strength = strengths(amplitudes, population, lower_symmetry, upper_symmetry, symmetry_pairs)
    lorentz = lorentz_widths(width_class, width_table, broadening)
    devices = lax.axis_size(("row", "col"))
    grid_total = float(GRID_DEV * devices)
    spectrum = by_lines(strength, lorentz, line_shard, line_bin, bin_offset, devices, grid_total)
    return (amplitudes, spectrum)


def solution(mesh):
    return jax.shard_map(
        shards,
        mesh=mesh,
        in_specs=(
            P("col", "row"),
            P("col", "row"),
            P(),
            P(None, "row"),
            P("row"),
            P("row"),
            P("row"),
            P("col"),
            P(),
            P("row", "col"),
            P(),
            P("row", "col"),
            P("row", "col"),
            P("row", "col"),
        ),
        out_specs=(P("row", "col"), P(("row", "col"))),
        check_vma=False,
    )
```

profile of v0, /device:TPU:0, one launch (start us, length us, event | category | flops | bytes accessed | tf_op | source)
XLA Modules:
  0.0 245.4 jit_solution(5967297606928048157)
XLA Ops:
  7.2 0.7 all-gather.2.cloned.1.call-update
  7.9 6.4 %copy.49 = bf16[128,16384]{0,1:T(8,128)(2,1)} copy(bf16[128,16384]{1,0:T(8,128)(2,1)} %param.23) | data formatting | bytes 8388608 | tf_op args[1]
  14.3 6.5 %copy.50 = bf16[128,64,256]{2,0,1:T(8,128)(2,1)} copy(bf16[128,64,256]{0,2,1:T(8,128)(2,1)} %bitcast.59) | data formatting | bytes 8388608 | tf_op jit(solution)/shard_map/reshape | solution.py:38
  20.8 0.9 fusion.66
  21.7 4.9 %collective-permute-start = (bf16[128,1,256]{2,0,1:T(8,128)(2,1)S(1)}, bf16[128,1,256]{2,0,1:T(8,128)(2,1)S(1)}, u32[]{:S(2)}, u32[]{:S(2)}) collective-permute-start(bf16[128,1,256]{2,0,1:T(8,128)(2,1)S(1)} %get-tuple-element.192), channel_id=1, source_target_pairs={{0,8},{8,16},{16,24},{1,9},{9,17},{17,25},{2,10},{10,18},{18,26},{... | collective-permute-start | bytes 196616 | tf_op jit(solution)/shard_map/ppermute | solution.py:24
  26.6 1.3 collective-permute-start.1
  28.0 6.7 %sort.17 = (s32[6144]{0:T(1024)}, s32[6144]{0:T(1024)S(1)}) sort(s32[6144]{0:T(1024)S(1)} %bitcast.56, s32[6144]{0:T(1024)S(1)} %iota.51), dimensions={0}, to_apply=%region_1.0 | sort | flops 79872 | bytes 98304 | tf_op jit(solution)/shard_map/jit(argsort)/sort | solution.py:105
  34.7 34.5 %gather_fusion = s32[6144]{0:T(1024)S(1)} fusion(s32[6144]{0:T(1024)S(1)} %bitcast.57, s32[6144]{0:T(1024)S(1)} %fusion.62), kind=kCustom, calls=%fused_computation | custom fusion | bytes 73728 | tf_op jit(solution)/shard_map/gather | solution.py:106
  69.2 0.1 slice_compare_fusion
  69.3 0.1 add_select_fusion.1
  69.4 0.3 reduce-window.9
  69.7 0.1 reduce-window.12
  69.9 11.0 %copy.70 = f32[4,24576]{0,1:T(8,128)} copy(f32[4,24576]{0,1:T(8,128)} %constant.263.clone.1) | data formatting | bytes 786432
  80.9 0.1 slice_reduce_fusion
  81.0 0.1 select_reduce_fusion
  81.3 1.3 fusion.55
  82.7 0.1 select_reduce_fusion.1
  82.8 0.7 copy-done.1
  83.5 1.3 fusion.42
  84.8 4.4 %add_convert_fusion = bf16[128,64,256]{2,0,1:T(8,128)(2,1)} fusion(f32[128,64,256]{2,0,1:T(8,128)S(1)} %fusion.55, f32[128,64,256]{2,0,1:T(8,128)S(1)} %fusion.42, f32[64]{0:T(128)S(1)} %get-tuple-element.196, f32[64]{0:T(128)S(1)} %get-tuple-element.197, f32[64]{0:T(128)S(1)} %get-tuple-element.195, bf16[128,1,256]{2,0,1:T(8,128)(2,1)S(1)} %collective-permute-done.1, ...), kind=kOutput, calls=%fused_computation.63 | convolution fusion | flops 1094844416 | bytes 25363968 | tf_op jit(solution)/shard_map/ukj,ij->uki/dot_general | solution.py:44
  89.2 6.4 %copy.55 = bf16[128,64,256]{0,2,1:T(8,128)(2,1)} copy(bf16[128,64,256]{2,0,1:T(8,128)(2,1)} %add_convert_fusion) | data formatting | bytes 8388608 | tf_op jit(solution)/shard_map/convert_element_type | solution.py:48
  95.6 6.5 %convolution_bitcast_fusion = f32[192,128]{1,0:T(8,128)} fusion(bf16[192,16384]{1,0:T(8,128)(2,1)} %all-gather.2.cloned.1.call-done, bf16[128,16384]{0,1:T(8,128)(2,1)} %bitcast.61), kind=kOutput, calls=%fused_computation.74 | convolution fusion | flops 805306368 | bytes 10584064 | tf_op jit(solution)/shard_map/dot_general | solution.py:159
  102.2 21.5 %reduce-scatter.2.cloned.1.call-done = f32[48,128]{1,0:T(8,128)} async-done(((f32[192,128]{1,0:T(8,128)}), f32[48,128]{1,0:T(8,128)}) %reduce-scatter.2.cloned.1.call-update) | async-done | bytes 24592 | tf_op jit(solution)/shard_map/reduce_scatter | solution.py:165
  123.6 0.8 fusion.61
  124.5 0.1 pad_maximum_fusion
  124.6 1.1 copy.56
  125.7 45.7 %scatter_custom_fusion = f32[4,24576]{0,1:T(8,128)} fusion(f32[4,24576]{0,1:T(8,128)} %copy.70, s32[6144]{0:T(1024)S(1)} %bitcast.75, f32[4,6144]{0,1:T(8,128)S(1)} %copy.56, s32[6144]{0:T(1024)S(1)} %fusion.62), kind=kCustom, calls=%fused_computation.72 | custom fusion | bytes 393216 | tf_op jit(solution)/shard_map/scatter | solution.py:120
  171.4 8.1 %copy.57 = f32[4,32,768]{2,0,1:T(4,128)} copy(f32[4,32,768]{0,2,1:T(8,128)} %bitcast.58) | data formatting | bytes 786432 | tf_op jit(solution)/shard_map/reshape | solution.py:120
  179.5 3.0 %all-to-all-start = ((f32[4,32,768]{2,0,1:T(4,128)}), f32[4,32,768]{2,0,1:T(4,128)S(1)}, u32[]{:S(2)}, u32[]{:S(2)}) async-start(f32[4,32,768]{2,0,1:T(4,128)} %copy.57), calls=%async_computation.1 | async-start | bytes 786432 | tf_op jit(solution)/shard_map/all_to_all | solution.py:126
  182.5 12.9 %all-to-all-done = f32[4,32,768]{2,0,1:T(4,128)S(1)} async-done(((f32[4,32,768]{2,0,1:T(4,128)}), f32[4,32,768]{2,0,1:T(4,128)S(1)}, u32[]{:S(2)}, u32[]{:S(2)}) %all-to-all-start) | async-done | bytes 393248 | tf_op jit(solution)/shard_map/all_to_all | solution.py:126
  195.5 0.1 copy.58
  195.6 0.1 reshape.386
  195.7 36.2 %while.19 = (s32[]{:T(128)}, f32[8320]{0:T(1024)S(1)}, f32[4,8,3072]{2,1,0:T(8,128)S(1)}, s32[]{:T(128)}, s32[]{:T(128)}, /*index=5*/s32[]{:T(128)}, s32[]{}, s32[]{}, s32[]{}) while((s32[]{:T(128)}, f32[8320]{0:T(1024)S(1)}, f32[4,8,3072]{2,1,0:T(8,128)S(1)}, s32[]{:T(128)}, s32[]{:T(128)}, /*index=5*/s32[]{:T(128)}, s32[]{}, s32[]{}, ...), condition=%wide.region_8.9_spmd.clone, body=%wide.region_7.8_spmd.clone.sunk | while | flops 619235712 | bytes 709791 | solution.py:135
  195.8 4.4 %fusion.74 = f32[64,256]{1,0:T(8,128)S(1)} fusion(f32[3072]{0:T(1024)S(1)} %get-tuple-element.241, f32[3072]{0:T(1024)S(1)} %get-tuple-element.242, f32[3072]{0:T(1024)S(1)} %get-tuple-element.243, f32[3072]{0:T(1024)S(1)} %get-tuple-element.244, f32[3072]{0:T(1024)S(1)} %bitcast.67, f32[3072]{0:T(1024)S(1)} %bitcast.65, ...), kind=kOutput, calls=%fused_computation.3.clone.1 | convolution fusion | flops 619118592 | bytes 188416 | tf_op jit(solution)/shard_map/while/body/eval_jaxpr/dot_general | solution.py:92
  200.3 4.4 %fusion.74 = f32[64,256]{1,0:T(8,128)S(1)} fusion(f32[3072]{0:T(1024)S(1)} %get-tuple-element.241, f32[3072]{0:T(1024)S(1)} %get-tuple-element.242, f32[3072]{0:T(1024)S(1)} %get-tuple-element.243, f32[3072]{0:T(1024)S(1)} %get-tuple-element.244, f32[3072]{0:T(1024)S(1)} %bitcast.67, f32[3072]{0:T(1024)S(1)} %bitcast.65, ...), kind=kOutput, calls=%fused_computation.3.clone.1 | convolution fusion | flops 619118592 | bytes 188416 | tf_op jit(solution)/shard_map/while/body/eval_jaxpr/dot_general | solution.py:92
  204.9 4.3 %fusion.74 = f32[64,256]{1,0:T(8,128)S(1)} fusion(f32[3072]{0:T(1024)S(1)} %get-tuple-element.241, f32[3072]{0:T(1024)S(1)} %get-tuple-element.242, f32[3072]{0:T(1024)S(1)} %get-tuple-element.243, f32[3072]{0:T(1024)S(1)} %get-tuple-element.244, f32[3072]{0:T(1024)S(1)} %bitcast.67, f32[3072]{0:T(1024)S(1)} %bitcast.65, ...), kind=kOutput, calls=%fused_computation.3.clone.1 | convolution fusion | flops 619118592 | bytes 188416 | tf_op jit(solution)/shard_map/while/body/eval_jaxpr/dot_general | solution.py:92
  209.4 4.3 %fusion.74 = f32[64,256]{1,0:T(8,128)S(1)} fusion(f32[3072]{0:T(1024)S(1)} %get-tuple-element.241, f32[3072]{0:T(1024)S(1)} %get-tuple-element.242, f32[3072]{0:T(1024)S(1)} %get-tuple-element.243, f32[3072]{0:T(1024)S(1)} %get-tuple-element.244, f32[3072]{0:T(1024)S(1)} %bitcast.67, f32[3072]{0:T(1024)S(1)} %bitcast.65, ...), kind=kOutput, calls=%fused_computation.3.clone.1 | convolution fusion | flops 619118592 | bytes 188416 | tf_op jit(solution)/shard_map/while/body/eval_jaxpr/dot_general | solution.py:92
  213.9 4.3 %fusion.74 = f32[64,256]{1,0:T(8,128)S(1)} fusion(f32[3072]{0:T(1024)S(1)} %get-tuple-element.241, f32[3072]{0:T(1024)S(1)} %get-tuple-element.242, f32[3072]{0:T(1024)S(1)} %get-tuple-element.243, f32[3072]{0:T(1024)S(1)} %get-tuple-element.244, f32[3072]{0:T(1024)S(1)} %bitcast.67, f32[3072]{0:T(1024)S(1)} %bitcast.65, ...), kind=kOutput, calls=%fused_computation.3.clone.1 | convolution fusion | flops 619118592 | bytes 188416 | tf_op jit(solution)/shard_map/while/body/eval_jaxpr/dot_general | solution.py:92
  218.4 4.4 %fusion.74 = f32[64,256]{1,0:T(8,128)S(1)} fusion(f32[3072]{0:T(1024)S(1)} %get-tuple-element.241, f32[3072]{0:T(1024)S(1)} %get-tuple-element.242, f32[3072]{0:T(1024)S(1)} %get-tuple-element.243, f32[3072]{0:T(1024)S(1)} %get-tuple-element.244, f32[3072]{0:T(1024)S(1)} %bitcast.67, f32[3072]{0:T(1024)S(1)} %bitcast.65, ...), kind=kOutput, calls=%fused_computation.3.clone.1 | convolution fusion | flops 619118592 | bytes 188416 | tf_op jit(solution)/shard_map/while/body/eval_jaxpr/dot_general | solution.py:92
  223.0 4.3 %fusion.74 = f32[64,256]{1,0:T(8,128)S(1)} fusion(f32[3072]{0:T(1024)S(1)} %get-tuple-element.241, f32[3072]{0:T(1024)S(1)} %get-tuple-element.242, f32[3072]{0:T(1024)S(1)} %get-tuple-element.243, f32[3072]{0:T(1024)S(1)} %get-tuple-element.244, f32[3072]{0:T(1024)S(1)} %bitcast.67, f32[3072]{0:T(1024)S(1)} %bitcast.65, ...), kind=kOutput, calls=%fused_computation.3.clone.1 | convolution fusion | flops 619118592 | bytes 188416 | tf_op jit(solution)/shard_map/while/body/eval_jaxpr/dot_general | solution.py:92
  227.5 4.3 %fusion.74 = f32[64,256]{1,0:T(8,128)S(1)} fusion(f32[3072]{0:T(1024)S(1)} %get-tuple-element.241, f32[3072]{0:T(1024)S(1)} %get-tuple-element.242, f32[3072]{0:T(1024)S(1)} %get-tuple-element.243, f32[3072]{0:T(1024)S(1)} %get-tuple-element.244, f32[3072]{0:T(1024)S(1)} %bitcast.67, f32[3072]{0:T(1024)S(1)} %bitcast.65, ...), kind=kOutput, calls=%fused_computation.3.clone.1 | convolution fusion | flops 619118592 | bytes 188416 | tf_op jit(solution)/shard_map/while/body/eval_jaxpr/dot_general | solution.py:92
  232.0 1.4 collective-permute-start.2
  233.4 0.1 slice.175
  233.4 0.7 collective-permute-done.2
  234.2 1.3 collective-permute-start.3
  235.5 2.2 collective-permute-done.3
  237.8 0.1 fusion.63
  237.9 0.6 copy-done.4
  (94 shorter events, 1.5 us)
Async XLA Ops:
  7.2 88.4 %all-gather.2.cloned.1.call-start = ((), (), s32[]{:S(2)}) async-start(), calls=%async_computation.2 | async-start | bytes 7077888 | tf_op jit(solution)/shard_map/all_gather | solution.py:160
  7.9 115.7 %reduce-scatter.2.cloned.1.call-start = ((), (), s32[]{:S(2)}) async-start(), calls=%async_computation.3 | async-start | bytes 122880 | tf_op jit(solution)/shard_map/reduce_scatter | solution.py:165
  14.3 13.6 %copy-start.6 = (s32[48,128]{1,0:T(8,128)S(1)}, s32[48,128]{1,0:T(8,128)}, u32[]{:S(2)}) copy-start(s32[48,128]{1,0:T(8,128)} %param.34) | copy-start | bytes 73732
  14.3 13.7 %copy-start = (s32[48,128]{1,0:T(8,128)S(1)}, s32[48,128]{1,0:T(8,128)}, u32[]{:S(2)}) copy-start(s32[48,128]{1,0:T(8,128)} %param.33) | copy-start | bytes 73732
  21.7 61.1 %collective-permute-start = (bf16[128,1,256]{2,0,1:T(8,128)(2,1)S(1)}, bf16[128,1,256]{2,0,1:T(8,128)(2,1)S(1)}, u32[]{:S(2)}, u32[]{:S(2)}) collective-permute-start(bf16[128,1,256]{2,0,1:T(8,128)(2,1)S(1)} %get-tuple-element.192), channel_id=1, source_target_pairs={{0,8},{8,16},{16,24},{1,9},{9,17},{17,25},{2,10},{10,18},{18,26},{... | collective-permute-start | bytes 196616 | tf_op jit(solution)/shard_map/ppermute | solution.py:24
  26.6 58.1 %collective-permute-start.1 = (bf16[128,1,256]{2,0,1:T(8,128)(2,1)S(1)}, bf16[128,1,256]{2,0,1:T(8,128)(2,1)S(1)}, u32[]{:S(2)}, u32[]{:S(2)}) collective-permute-start(bf16[128,1,256]{2,0,1:T(8,128)(2,1)S(1)} %get-tuple-element.191), channel_id=1, source_target_pairs={{8,0},{16,8},{24,16},{9,1},{17,9},{25,17},{10,2},{18,10},{26,18},{... | collective-permute-start | bytes 196616 | tf_op jit(solution)/shard_map/ppermute | solution.py:25
  69.8 11.2 %copy-start.7 = (s32[48,128]{1,0:T(8,128)S(1)}, s32[48,128]{1,0:T(8,128)}, u32[]{:S(2)}) copy-start(s32[48,128]{1,0:T(8,128)} %param.31) | copy-start | bytes 73732
  69.8 11.2 %copy-start.9 = (f32[8]{0:T(128)S(1)}, f32[8]{0:T(128)}, u32[]{:S(2)}) copy-start(f32[8]{0:T(128)} %param.32) | copy-start | bytes 100
  69.8 11.3 %copy-start.8 = (f32[3,64]{1,0:T(4,128)S(1)}, f32[3,64]{1,0:T(4,128)}, u32[]{:S(2)}) copy-start(f32[3,64]{1,0:T(4,128)} %param.25) | copy-start | bytes 2308
  69.9 11.4 %copy-start.2 = (bf16[128,16384]{0,1:T(8,128)(2,1)S(1)}, bf16[128,16384]{0,1:T(8,128)(2,1)}, u32[]{:S(2)}) copy-start(bf16[128,16384]{0,1:T(8,128)(2,1)} %copy.49) | copy-start | bytes 12582916
  69.9 11.4 %copy-start.3 = (bf16[3,256,256]{2,1,0:T(8,128)(2,1)S(1)}, bf16[3,256,256]{2,1,0:T(8,128)(2,1)}, u32[]{:S(2)}) copy-start(bf16[3,256,256]{2,1,0:T(8,128)(2,1)} %param.24) | copy-start | bytes 1179652
  81.3 1.4 copy-start.13
  81.3 1.4 copy-start.14
  81.3 2.2 copy-start.1
  95.6 6.5 %copy-start.10 = (f32[48]{0:T(128)S(1)}, f32[48]{0:T(128)}, u32[]{:S(2)}) copy-start(f32[48]{0:T(128)} %param.27) | copy-start | bytes 580
  95.6 28.1 %copy-start.11 = (f32[48]{0:T(128)S(1)}, f32[48]{0:T(128)}, u32[]{:S(2)}) copy-start(f32[48]{0:T(128)} %param.26) | copy-start | bytes 580
  95.6 28.1 %copy-start.12 = (s32[128]{0:T(128)S(1)}, s32[128]{0:T(128)}, u32[]{:S(2)}) copy-start(s32[128]{0:T(128)} %param.29) | copy-start | bytes 1540
  95.6 28.9 %copy-start.5 = (f32[48,128]{1,0:T(8,128)S(1)}, f32[48,128]{1,0:T(8,128)}, u32[]{:S(2)}) copy-start(f32[48,128]{1,0:T(8,128)} %param.35) | copy-start | bytes 73732
  179.5 16.0 %all-to-all-start = ((f32[4,32,768]{2,0,1:T(4,128)}), f32[4,32,768]{2,0,1:T(4,128)S(1)}, u32[]{:S(2)}, u32[]{:S(2)}) async-start(f32[4,32,768]{2,0,1:T(4,128)} %copy.57), calls=%async_computation.1 | async-start | bytes 786432 | tf_op jit(solution)/shard_map/all_to_all | solution.py:126
  232.0 2.2 collective-permute-start.2
  234.2 3.5 %collective-permute-start.3 = (f32[64]{0:T(128)S(1)}, f32[64]{0:T(128)S(1)}, u32[]{:S(2)}, u32[]{:S(2)}) collective-permute-start(f32[64]{0:T(128)S(1)} %get-tuple-element.193), channel_id=1, source_target_pairs={{1,0},{2,1},{3,2},{4,3},{5,4},{6,5},{7,6},{8,7},{9,8},{10,9},{11,1... | collective-permute-start | bytes 776 | tf_op jit(solution)/shard_map/ppermute | solution.py:33
  237.9 0.6 copy-start.4
Sparse Core Ops, SparseCore 0:
  9.9 48.6 all-gather.1
  102.2 21.3 reduce-scatter.1
where the time goes:
time: 250 us; the launch traced here: 245 us
  local copies, waits for them, and re-layouts  123 us (49%)
  matrix products  48.3 us (19%)
  waiting for transfers between devices  38.1 us (15%)
  between operations  14.4 us (6%)
  starting transfers between devices  11.9 us (5%)
  other arithmetic  9.61 us (4%)
    scatter x1, local copies, waits for them, and re-layouts, pack_lines(): return filler.at[:, slot_index].set(payload).reshape(4, devices, capacity)  45.7 us
    dot_general x8, matrix products, tile_binning(): jnp.dot(onehot, windows, precision=lax.Precision.HIGHEST, preferred_eleme...  34.8 us
    gather x1, local copies, waits for them, and re-layouts, pack_lines(): sorted_owner = line_owner[line_order]  34.5 us
    reduce_scatter x1, waiting for transfers between devices, shards(): lax.psum_scatter(partial_value, 'row', scatter_dimension=0, tiled=True)  21.5 us
    unnamed x32, local copies, waits for them, and re-layouts  18.8 us
    all_to_all x1, waiting for transfers between devices, by_lines(): lax.all_to_all(outgoing, ('row', 'col'), split_axis=1, concat_axis=1, til...  12.9 us
    reshape x1, local copies, waits for them, and re-layouts, pack_lines(): return filler.at[:, slot_index].set(payload).reshape(4, devices, capacity)  8.12 us
    dot_general x3, matrix products, apply_dipole(): jnp.einsum('ukj,ij->uki', shifted, vib_dipole[band_index], preferred_elem...  6.99 us
  transfers between devices with their start and end apart: 7, of which 4 were waited for; matrix products, arithmetic and copies ran while one was open for 33% of the time, Pallas kernels for 0%

commit v1 on v0

v1 whole, which is shorter than its diff:
```python
import functools
import math

import jax
import jax.numpy as jnp
from jax import lax
from jax.experimental import pallas as pl
from jax.experimental.pallas import tpu as pltpu
from jax.sharding import PartitionSpec as P

NV = 256
HW = 64
GRID_DEV = 8192
LANE = 128
TILES_DEV = GRID_DEV // LANE
GROUP = 4
MESH = pl.DeviceIdType.MESH

doppler_base = 1.5
log_two = math.log(2.0)

f32 = jnp.float32
bf16 = jnp.bfloat16


def flip(index, mask):
    bit = 1
    while bit <= mask:
        if mask & bit:
            index = index + bit - 2 * bit * ((index // bit) % 2)
        bit *= 2
    return index


def iota(shape, dim):
    return lax.broadcasted_iota(jnp.int32, shape, dim)


def column_of(row_value):
    n = row_value.shape[1]
    eye = iota((n, n), 0) == iota((n, n), 1)
    return jnp.sum(jnp.where(eye, row_value, jnp.zeros_like(row_value)), axis=1, keepdims=True)


def kernel(
    nrow,
    ncol,
    lower_ref,
    upper_ref,
    vib_ref,
    rot_ref,
    population_ref,
    broadening_ref,
    lower_sym_ref,
    upper_sym_ref,
    pairs_ref,
    width_class_ref,
    table_ref,
    shard_ref,
    bin_ref,
    offset_ref,
    amp_ref,
    spec_ref,
    padded,
    weighted,
    gathered,
    partial,
    amp_in,
    coef,
    place,
    unit,
    windows,
    onehot,
    outgoing,
    incoming,
    totals,
    arrived,
    local_sem,
    halo_send,
    halo_recv,
    gather_send,
    gather_recv,
    amp_send,
    amp_recv,
    col_send,
    col_recv,
    row_send,
    row_recv,
):
    row = lax.axis_index("row")
    col = lax.axis_index("col")
    uppers, basis = upper_ref.shape
    slabs = basis // NV
    two, pair_rows, piece = lower_ref.shape
    lows = pair_rows // 2
    low_rows, lines = bin_ref.shape
    tiles = nrow * ncol * TILES_DEV
    chunk = ncol * TILES_DEV
    bits = []
    bit = ncol // 2
    while bit:
        bits.append(bit)
        bit //= 2
    orders = [bits, [bits[1], bits[0]] + bits[2:]]

    load = pltpu.make_async_copy(upper_ref, padded.at[:, pl.ds(NV, basis)], local_sem.at[0])
    load.start()
    own = pltpu.make_async_copy(lower_ref, gathered.at[:, pl.ds(0, pair_rows)], local_sem.at[1])
    own.start()

    barrier = pltpu.get_barrier_semaphore()
    for d in range(1, ncol):
        pl.semaphore_signal(
            barrier, inc=1, device_id=(row, (col + d) % ncol), device_id_type=MESH
        )
    for d in range(1, nrow):
        pl.semaphore_signal(
            barrier, inc=1, device_id=((row + d) % nrow, col), device_id_type=MESH
        )
    pl.semaphore_wait(barrier, ncol + nrow - 2)

    def piece_copy(half, mask, bit):
        if mask == 0:
            src = lower_ref.at[half]
        else:
            src = gathered.at[half, pl.ds(mask * pair_rows, pair_rows)]
        to = mask ^ bit
        return pltpu.make_async_remote_copy(
            src_ref=src,
            dst_ref=gathered.at[half, pl.ds(to * pair_rows, pair_rows)],
            send_sem=gather_send.at[half, to],
            recv_sem=gather_recv.at[half, to],
            device_id=(row, flip(col, bit)),
            device_id_type=MESH,
        )

    up = pltpu.make_async_remote_copy(
        src_ref=upper_ref.at[:, pl.ds(basis - NV, NV)],
        dst_ref=padded.at[:, pl.ds(0, NV)],
        send_sem=halo_send.at[0],
        recv_sem=halo_recv.at[0],
        device_id=((row + 1) % nrow, col),
        device_id_type=MESH,
    )
    down = pltpu.make_async_remote_copy(
        src_ref=upper_ref.at[:, pl.ds(0, NV)],
        dst_ref=padded.at[:, pl.ds(basis + NV, NV)],
        send_sem=halo_send.at[1],
        recv_sem=halo_recv.at[1],
        device_id=((row + nrow - 1) % nrow, col),
        device_id_type=MESH,
    )
    pl.when(row < nrow - 1)(lambda: up.start())
    pl.when(row > 0)(lambda: down.start())

    started = []

    def send(half, mask, bit):
        copy = piece_copy(half, mask, bit)
        copy.start()
        started.append(copy)

    for level in range(len(bits)):
        for half in range(2):
            send(half, 0, orders[half][level])

    broad = column_of(broadening_ref[...])
    width_class = width_class_ref[...]
    lorentz = jnp.zeros(width_class.shape, f32)
    for i in range(table_ref.shape[0]):
        lorentz = lorentz + jnp.where(width_class == i, table_ref[i], 0.0)
    lorentz = lorentz * broad
    position = shard_ref[...] * GRID_DEV + bin_ref[...]
    center = position.astype(f32) + offset_ref[...]
    doppler = doppler_base * (1.0 + center / float(GRID_DEV * nrow * ncol))
    mixing = lorentz / (lorentz + doppler)
    coef[0] = mixing * lorentz / math.pi
    coef[1] = lorentz * lorentz
    coef[2] = (1.0 - mixing) * (math.sqrt(log_two / math.pi) / doppler)
    coef[3] = -log_two / (doppler * doppler)
    coef[4] = offset_ref[...]
    start = position - HW
    place[0] = lax.shift_right_arithmetic(start, 7)
    place[1] = lax.bitwise_and(start, LANE - 1)

    load.wait()

    @pl.when(row == 0)
    def _():
        padded[:, pl.ds(0, NV)] = jnp.zeros((uppers, NV), bf16)

    @pl.when(row == nrow - 1)
    def _():
        padded[:, pl.ds(basis + NV, NV)] = jnp.zeros((uppers, NV), bf16)

    pl.when(row > 0)(lambda: up.wait_recv())
    pl.when(row < nrow - 1)(lambda: down.wait_recv())

    half_slabs = slabs // 2

    def weigh(g, _):
        first = g * GROUP
        sums = [jnp.zeros((uppers, NV), f32) for _ in range(GROUP)]
        for band in range(3):
            blocks = [
                padded[:, pl.ds(pl.multiple_of((first + j + band) * NV, NV), NV)]
                for j in range(GROUP)
            ]
            product = lax.dot_general(
                jnp.concatenate(blocks, axis=0),
                vib_ref[band],
                (((1,), (1,)), ((), ())),
                preferred_element_type=f32,
            )
            for j in range(GROUP):
                sums[j] = sums[j] + rot_ref[band, first + j] * product[j * uppers : (j + 1) * uppers]
        part = first // half_slabs
        for j in range(GROUP):
            at = pl.multiple_of((first + j - part * half_slabs) * NV, NV)
            weighted[pl.ds(pl.multiple_of(part * uppers, uppers), uppers), pl.ds(at, NV)] = sums[
                j
            ].astype(bf16)
        return 0

    lax.fori_loop(0, slabs // GROUP, weigh, 0)

    def slots_of(half, level):
        order = orders[half]
        masks = [0]
        for b in order[:level]:
            masks = masks + [m ^ b for m in masks]
        return [(m, m ^ order[level]) for m in masks]

    def forward(level):
        count = len(slots_of(0, level))
        for i in range(count):
            for half in range(2):
                mask, slot = slots_of(half, level)[i]
                piece_copy(half, mask, orders[half][level]).wait_recv()
                for later in orders[half][level + 1 :]:
                    send(half, slot, later)

    forward(0)

    cell = iota((LANE, lines), 0)

    def shape_row(r, _):
        inside = place[1, pl.ds(r, 1), :]
        step = lax.bitwise_and(cell - inside, LANE - 1) - HW
        x = step.astype(f32) - coef[4, pl.ds(r, 1), :]
        square = x * x
        unit[r] = coef[0, pl.ds(r, 1), :] / (square + coef[1, pl.ds(r, 1), :]) + coef[
            2, pl.ds(r, 1), :
        ] * jnp.exp(coef[3, pl.ds(r, 1), :] * square)
        return 0

    lax.fori_loop(0, low_rows, shape_row, 0)

    tile_iota = iota((chunk, lines), 0)

    def build(m, slot):
        def build_row(r, _):
            tile = place[0, pl.ds(r, 1), :]
            tile = jnp.where(tile < 0, tile + tiles, tile) - m * chunk
            hit = jnp.where(tile_iota == tile, 1.0, 0.0).astype(bf16)
            onehot[slot, :, pl.ds(pl.multiple_of(r * lines, lines), lines)] = hit
            return 0

        lax.fori_loop(0, low_rows, build_row, 0)

    early = onehot.shape[0] == nrow
    split = nrow // 2
    if early:
        lax.fori_loop(0, split, lambda m, _: (build(m, m), 0)[1], 0)
    for level in range(1, len(bits) - 1):
        forward(level)
    if early:
        lax.fori_loop(split, nrow, lambda m, _: (build(m, m), 0)[1], 0)
    forward(len(bits) - 1)
    own.wait()

    total = jnp.zeros((ncol * pair_rows, 2 * uppers), f32)
    for half in range(2):
        total = total + lax.dot_general(
            gathered[half],
            weighted[:, pl.ds(half * piece, piece)],
            (((1,), (1,)), ((), ())),
            preferred_element_type=f32,
        )
    for mask in range(ncol):
        base = mask * pair_rows
        rows = total[base : base + lows, :uppers] + total[base + lows : base + 2 * lows, uppers:]
        partial[pl.ds(pl.multiple_of(flip(col, mask) * lows, 8), lows), :] = rows

    def amp_rows(owner):
        return partial.at[pl.ds(pl.multiple_of(owner * low_rows, 8), low_rows)]

    amp_copies = []
    for d in range(1, nrow):
        to = (row + d) % nrow
        copy = pltpu.make_async_remote_copy(
            src_ref=amp_rows(to),
            dst_ref=amp_in.at[d - 1],
            send_sem=amp_send.at[d - 1],
            recv_sem=amp_recv.at[d - 1],
            device_id=(to, col),
            device_id_type=MESH,
        )
        copy.start()
        amp_copies.append(copy)
    population = column_of(population_ref[...])
    lower_sym = lower_sym_ref[...]
    allowed = jnp.zeros(lower_sym.shape, jnp.int32)
    for i in range(pairs_ref.shape[0]):
        allowed = allowed + jnp.where(lower_sym == i, pairs_ref[i], 0)
    allowed = column_of(allowed)
    keep = jnp.where(upper_sym_ref[...] == allowed, 1.0, 0.0)
    amplitudes = partial[pl.ds(pl.multiple_of(row * low_rows, 8), low_rows), :]
    for d in range(1, nrow):
        amp_copies[d - 1].wait_recv()
        amplitudes = amplitudes + amp_in[d - 1]
    amp_ref[...] = amplitudes
    coef[5] = population * amplitudes * amplitudes * keep

    def scale_row(r, before):
        inside = place[1, pl.ds(r, 1), :]
        tile = place[0, pl.ds(r, 1), :]
        value = unit[r] * coef[5, pl.ds(r, 1), :]
        is_head = cell >= inside
        head = jnp.where(is_head & (tile >= 0), value, 0.0)
        tail = jnp.where(is_head | (tile >= tiles - 1), 0.0, value)
        lane = pl.ds(pl.multiple_of(r * lines, lines), lines)
        windows[pl.ds(0, LANE), lane] = head.astype(bf16)
        windows[pl.ds(LANE, LANE), lane] = tail.astype(bf16)
        return before + jnp.where(tile < 0, tail, 0.0)

    before = lax.fori_loop(0, low_rows, scale_row, jnp.zeros((LANE, lines), f32))
    before = jnp.sum(before, axis=1, keepdims=True)
    eye = iota((LANE, LANE), 0) == iota((LANE, LANE), 1)
    carry = jnp.sum(jnp.where(eye, before, 0.0), axis=0, keepdims=True)
    first_row = iota((chunk, LANE), 0) == 0

    def col_copy(d, m):
        to = (col + d) % ncol
        return pltpu.make_async_remote_copy(
            src_ref=outgoing.at[m, to],
            dst_ref=incoming.at[m, d - 1],
            send_sem=col_send.at[m, d - 1],
            recv_sem=col_recv.at[m, d - 1],
            device_id=(row, to),
            device_id_type=MESH,
        )

    def bin_chunk(m, carry):
        if not early:
            build(m, 0)
        slot = m if early else 0
        product = lax.dot_general(
            onehot[slot], windows[...], (((1,), (1,)), ((), ())), preferred_element_type=f32
        )
        tail = product[:, LANE:]
        shifted = jnp.where(first_row, carry, pltpu.roll(tail, 1, 0))
        cells = product[:, :LANE] + shifted
        outgoing[m] = cells.astype(bf16).reshape(ncol, TILES_DEV, LANE)
        for d in range(1, ncol):
            col_copy(d, m).start()
        return tail[chunk - 1 :, :]

    lax.fori_loop(0, nrow, bin_chunk, carry)

    def add_chunk(m, _):
        value = outgoing[m, col].astype(f32)
        for d in range(1, ncol):
            col_copy(d, m).wait_recv()
            value = value + incoming[m, d - 1].astype(f32)
        totals[m] = value
        return 0

    lax.fori_loop(0, nrow, add_chunk, 0)
    row_copies = []
    for d in range(1, nrow):
        to = (row + d) % nrow
        copy = pltpu.make_async_remote_copy(
            src_ref=totals.at[to],
            dst_ref=arrived.at[d - 1],
            send_sem=row_send.at[d - 1],
            recv_sem=row_recv.at[d - 1],
            device_id=(to, col),
            device_id_type=MESH,
        )
        copy.start()
        row_copies.append(copy)
    value = totals[row]
    for d in range(1, nrow):
        row_copies[d - 1].wait_recv()
        value = value + arrived[d - 1]
    spec_ref[...] = value

    for copy in started + amp_copies + row_copies:
        copy.wait_send()

    def drain(m, _):
        for d in range(1, ncol):
            col_copy(d, m).wait_send()
        return 0

    lax.fori_loop(0, nrow, drain, 0)
    pl.when(row < nrow - 1)(lambda: up.wait_send())
    pl.when(row > 0)(lambda: down.wait_send())


def shards(
    lower_vectors,
    upper_vectors,
    vib_dipole,
    rot_factor,
    population,
    broadening,
    lower_symmetry,
    upper_symmetry,
    symmetry_pairs,
    width_class,
    width_table,
    line_shard,
    line_bin,
    bin_offset,
):
    nrow, ncol = lax.axis_size("row"), lax.axis_size("col")
    lows, basis = lower_vectors.shape
    uppers = upper_vectors.shape[0]
    low_rows, lines = line_bin.shape
    quarter = basis // 4
    pieces = lower_vectors.reshape(lows, 2, 2, quarter).transpose(2, 1, 0, 3)
    pieces = pieces.reshape(2, 2 * lows, quarter)
    chunk = ncol * TILES_DEV
    count = low_rows * lines
    early = nrow * chunk * count * 2 <= 26 * 2**20
    vmem = pl.BlockSpec(memory_space=pltpu.VMEM)
    smem = pl.BlockSpec(memory_space=pltpu.SMEM)
    hbm = pl.BlockSpec(memory_space=pl.ANY)
    dma = pltpu.SemaphoreType.DMA
    amplitudes, spectrum = pl.pallas_call(
        functools.partial(kernel, nrow, ncol),
        out_shape=(
            jax.ShapeDtypeStruct((low_rows, lines), f32),
            jax.ShapeDtypeStruct((TILES_DEV, LANE), f32),
        ),
        in_specs=[hbm, hbm, vmem, smem, vmem, vmem, vmem, vmem, smem, vmem, smem, vmem, vmem, vmem],
        out_specs=(vmem, vmem),
        scratch_shapes=[
            pltpu.VMEM((uppers, basis + 2 * NV), bf16),
            pltpu.VMEM((2 * uppers, basis // 2), bf16),
            pltpu.VMEM((2, ncol * 2 * lows, quarter), bf16),
            pltpu.VMEM((ncol * lows, uppers), f32),
            pltpu.VMEM((nrow - 1, low_rows, lines), f32),
            pltpu.VMEM((6, low_rows, lines), f32),
            pltpu.VMEM((2, low_rows, lines), jnp.int32),
            pltpu.VMEM((low_rows, LANE, lines), f32),
            pltpu.VMEM((2 * LANE, count), bf16),
            pltpu.VMEM((nrow if early else 1, chunk, count), bf16),
            pltpu.VMEM((nrow, ncol, TILES_DEV, LANE), bf16),
            pltpu.VMEM((nrow, ncol - 1, TILES_DEV, LANE), bf16),
            pltpu.VMEM((nrow, TILES_DEV, LANE), f32),
            pltpu.VMEM((nrow - 1, TILES_DEV, LANE), f32),
            dma((2,)),
            dma((2,)),
            dma((2,)),
            dma((2, ncol)),
            dma((2, ncol)),
            dma((nrow - 1,)),
            dma((nrow - 1,)),
            dma((nrow, ncol - 1)),
            dma((nrow, ncol - 1)),
            dma((nrow - 1,)),
            dma((nrow - 1,)),
        ],
        compiler_params=pltpu.CompilerParams(
            collective_id=0, has_side_effects=True, vmem_limit_bytes=58 * 2**20
        ),
    )(
        pieces,
        upper_vectors,
        vib_dipole,
        rot_factor,
        population[None, :],
        broadening[None, :],
        lower_symmetry[None, :],
        upper_symmetry[None, :],
        symmetry_pairs,
        width_class,
        width_table,
        line_shard,
        line_bin,
        bin_offset,
    )
    return (amplitudes, spectrum.reshape(GRID_DEV))


def solution(mesh):
    return jax.shard_map(
        shards,
        mesh=mesh,
        in_specs=(
            P("col", "row"),
            P("col", "row"),
            P(),
            P(None, "row"),
            P("row"),
            P("row"),
            P("row"),
            P("col"),
            P(),
            P("row", "col"),
            P(),
            P("row", "col"),
            P("row", "col"),
            P("row", "col"),
        ),
        out_specs=(P("row", "col"), P(("row", "col"))),
        check_vma=False,
    )
```

time: 250 us -> 69.7 us (0.28); the launches traced: 245 us -> 69.5 us
  local copies, waits for them, and re-layouts: 123 us -> 6.6 us
  Pallas kernels: 0 us -> 62.2 us
  matrix products: 48.3 us -> 0 us
  waiting for transfers between devices: 38.1 us -> 0 us
  between operations: 14.4 us -> 0.65 us
  starting transfers between devices: 11.9 us -> 0 us
  other arithmetic: 9.61 us -> 0 us
    pallas_call x0 -> x1, Pallas kernels: none -> 62.2 us  [shards(): pl.pallas_call(functools.partial(kernel, nrow, ncol), out_shape=(jax.Shap...]
    dot_general x12 -> x0, matrix products: 48.3 us -> none  [the longest x8 34.8 us: tile_binning(): jnp.dot(onehot, windows, precision=lax.Precision.HIGHEST, preferred_eleme...]
    scatter x1 -> x0, local copies, waits for them, and re-layouts: 45.7 us -> none  [pack_lines(): return filler.at[:, slot_index].set(payload).reshape(4, devices, capacity)]
    gather x1 -> x0, local copies, waits for them, and re-layouts: 34.5 us -> none  [pack_lines(): sorted_owner = line_owner[line_order]]
    reduce_scatter x1 -> x0, waiting for transfers between devices: 21.5 us -> none  [shards(): lax.psum_scatter(partial_value, 'row', scatter_dimension=0, tiled=True)]
    unnamed x32 -> x2, local copies, waits for them, and re-layouts: 18.8 us -> 2.72 us
    all_to_all x1 -> x0, waiting for transfers between devices: 12.9 us -> none  [by_lines(): lax.all_to_all(outgoing, ('row', 'col'), split_axis=1, concat_axis=1, til...]
    reshape x11 -> x2, local copies, waits for them, and re-layouts: 14.8 us -> 3.88 us  [shards(): pieces = lower_vectors.reshape(lows, 2, 2, quarter).transpose(2, 1, 0, 3)]
  transfers between devices with their start and end apart: 7 -> 0, of which waited for: 4 -> 0; matrix products, arithmetic and copies ran while one was open for 33% -> 0% of each run, Pallas kernels for 0% -> 0%
where the time goes in v1:
time: 69.7 us; the launch traced here: 69.5 us
  Pallas kernels  62.2 us (89%)
  local copies, waits for them, and re-layouts  6.6 us (9%)
    pallas_call x1, Pallas kernels, shards(): pl.pallas_call(functools.partial(kernel, nrow, ncol), out_shape=(jax.Shap...  62.2 us
    reshape x2, local copies, waits for them, and re-layouts, shards(): pieces = lower_vectors.reshape(lows, 2, 2, quarter).transpose(2, 1, 0, 3)  3.88 us
    unnamed x2, local copies, waits for them, and re-layouts  2.72 us

profile of v1, /device:TPU:0, one launch (start us, length us, event | category | flops | bytes accessed | tf_op | source)
XLA Modules:
  0.0 69.5 jit_solution(11940207430212682087)
XLA Ops:
  0.6 2.6 %reshape.13 = bf16[24,2,2,4096]{3,2,1,0:T(2,128)(2,1)S(1)} reshape(bf16[24,16384]{1,0:T(8,128)(2,1)} %param.14) | data formatting | bytes 1572864 | tf_op jit(solution)/shard_map/reshape | solution.py:433
  3.2 1.3 %copy.16 = bf16[24,2,2,4096]{3,0,1,2:T(8,128)(2,1)} copy(bf16[24,2,2,4096]{3,2,1,0:T(2,128)(2,1)S(1)} %reshape.13) | data formatting | bytes 1572864 | tf_op jit(solution)/shard_map/reshape | solution.py:433
  4.5 62.2 %shard_map.149 = (f32[48,128]{1,0:T(8,128)}, f32[64,128]{1,0:T(8,128)}) custom-call(bf16[2,48,4096]{2,1,0:T(8,128)(2,1)} %bitcast.8, bf16[128,16384]{1,0:T(8,128)(2,1)} %upper_ref.1, bf16[3,256,256]{2,1,0:T(8,128)(2,1)} %vib_ref.1, f32[3,64]{1,0:T(4,128)} %rot_ref.1, f32[1,48]{1,0:T(1,128)} %bitcast.10, f32[1,48]{1,0:T(1,128)} %bitcast.11, ...), custom_call_target="tpu_custom_call" | custom-call | tf_op jit(solution)/shard_map/pallas_call | solution.py:442
  66.7 1.3 %copy.19 = f32[48,128]{1,0:T(8,128)} copy(f32[48,128]{1,0:T(8,128)} %get-tuple-element.8) | data formatting | bytes 49152
  68.1 1.4 %copy.20 = f32[8192]{0:T(1024)} copy(f32[8192]{0:T(1024)} %bitcast.9) | data formatting | bytes 65536

commit v2 on v1

--- a/solution.py
+++ b/solution.py
@@ -119,15 +119,19 @@
         )
     pl.semaphore_wait(barrier, ncol + nrow - 2)
 
+    def slot_rows(mask):
+        at = mask // 2 + (mask % 2) * (ncol // 2)
+        return pl.ds(at * pair_rows, pair_rows)
+
     def piece_copy(half, mask, bit):
         if mask == 0:
             src = lower_ref.at[half]
         else:
-            src = gathered.at[half, pl.ds(mask * pair_rows, pair_rows)]
+            src = gathered.at[half, slot_rows(mask)]
         to = mask ^ bit
         return pltpu.make_async_remote_copy(
             src_ref=src,
-            dst_ref=gathered.at[half, pl.ds(to * pair_rows, pair_rows)],
+            dst_ref=gathered.at[half, slot_rows(to)],
             send_sem=gather_send.at[half, to],
             recv_sem=gather_recv.at[half, to],
             device_id=(row, flip(col, bit)),
@@ -183,6 +187,36 @@
     place[0] = lax.shift_right_arithmetic(start, 7)
     place[1] = lax.bitwise_and(start, LANE - 1)
 
+    cell = iota((LANE, lines), 0)
+
+    def shape_row(r, _):
+        inside = place[1, pl.ds(r, 1), :]
+        step = lax.bitwise_and(cell - inside, LANE - 1) - HW
+        x = step.astype(f32) - coef[4, pl.ds(r, 1), :]
+        square = x * x
+        unit[r] = coef[0, pl.ds(r, 1), :] / (square + coef[1, pl.ds(r, 1), :]) + coef[
+            2, pl.ds(r, 1), :
+        ] * jnp.exp(coef[3, pl.ds(r, 1), :] * square)
+        return 0
+
+    lax.fori_loop(0, low_rows, shape_row, 0)
+
+    tile_iota = iota((chunk, lines), 0)
+
+    def build(m, slot):
+        def build_row(r, _):
+            tile = place[0, pl.ds(r, 1), :]
+            tile = jnp.where(tile < 0, tile + tiles, tile) - m * chunk
+            hit = jnp.where(tile_iota == tile, 1.0, 0.0).astype(bf16)
+            onehot[slot, :, pl.ds(pl.multiple_of(r * lines, lines), lines)] = hit
+            return 0
+
+        lax.fori_loop(0, low_rows, build_row, 0)
+
+    early = onehot.shape[0] == nrow
+    if early:
+        lax.fori_loop(0, nrow, lambda m, _: (build(m, m), 0)[1], 0)
+
     load.wait()
 
     @pl.when(row == 0)
@@ -192,9 +226,6 @@
     @pl.when(row == nrow - 1)
     def _():
         padded[:, pl.ds(basis + NV, NV)] = jnp.zeros((uppers, NV), bf16)
-
-    pl.when(row > 0)(lambda: up.wait_recv())
-    pl.when(row < nrow - 1)(lambda: down.wait_recv())
 
     half_slabs = slabs // 2
 
@@ -222,7 +253,12 @@
             ].astype(bf16)
         return 0
 
-    lax.fori_loop(0, slabs // GROUP, weigh, 0)
+    def weigh_half(part):
+        steps = half_slabs // GROUP
+        lax.fori_loop(part * steps, (part + 1) * steps, weigh, 0)
+
+    pl.when(row > 0)(lambda: up.wait_recv())
+    weigh_half(0)
 
     def slots_of(half, level):
         order = orders[half]
@@ -231,9 +267,9 @@
             masks = masks + [m ^ b for m in masks]
         return [(m, m ^ order[level]) for m in masks]
 
-    def forward(level):
+    def forward(level, begin=0, end=None):
         count = len(slots_of(0, level))
-        for i in range(count):
+        for i in range(begin, count if end is None else end):
             for half in range(2):
                 mask, slot = slots_of(half, level)[i]
                 piece_copy(half, mask, orders[half][level]).wait_recv()
@@ -241,73 +277,49 @@
                     send(half, slot, later)
 
     forward(0)
-
-    cell = iota((LANE, lines), 0)
-
-    def shape_row(r, _):
-        inside = place[1, pl.ds(r, 1), :]
-        step = lax.bitwise_and(cell - inside, LANE - 1) - HW
-        x = step.astype(f32) - coef[4, pl.ds(r, 1), :]
-        square = x * x
-        unit[r] = coef[0, pl.ds(r, 1), :] / (square + coef[1, pl.ds(r, 1), :]) + coef[
-            2, pl.ds(r, 1), :
-        ] * jnp.exp(coef[3, pl.ds(r, 1), :] * square)
-        return 0
-
-    lax.fori_loop(0, low_rows, shape_row, 0)
-
-    tile_iota = iota((chunk, lines), 0)
-
-    def build(m, slot):
-        def build_row(r, _):
-            tile = place[0, pl.ds(r, 1), :]
-            tile = jnp.where(tile < 0, tile + tiles, tile) - m * chunk
-            hit = jnp.where(tile_iota == tile, 1.0, 0.0).astype(bf16)
-            onehot[slot, :, pl.ds(pl.multiple_of(r * lines, lines), lines)] = hit
-            return 0
-
-        lax.fori_loop(0, low_rows, build_row, 0)
-
-    early = onehot.shape[0] == nrow
-    split = nrow // 2
-    if early:
-        lax.fori_loop(0, split, lambda m, _: (build(m, m), 0)[1], 0)
-    for level in range(1, len(bits) - 1):
+    forward(1, 0, 1)
+    pl.when(row < nrow - 1)(lambda: down.wait_recv())
+
+    weigh_half(1)
+    forward(1, 1)
+    for level in range(2, len(bits) - 1):
         forward(level)
-    if early:
-        lax.fori_loop(split, nrow, lambda m, _: (build(m, m), 0)[1], 0)
+    own.wait()
+
+    side = ncol // 2 * pair_rows
+    amp_copies = []
+
+    def sum_half(odd):
+        total = jnp.zeros((side, 2 * uppers), f32)
+        for half in range(2):
+            total = total + lax.dot_general(
+                gathered[half, pl.ds(odd * side, side)],
+                weighted[:, pl.ds(half * piece, piece)],
+                (((1,), (1,)), ((), ())),
+                preferred_element_type=f32,
+            )
+        for i in range(ncol // 2):
+            base = i * pair_rows
+            rows = total[base : base + lows, :uppers] + total[base + lows : base + 2 * lows, uppers:]
+            source = flip(col, 2 * i + odd)
+            partial[pl.ds(pl.multiple_of(source * lows, 8), lows), :] = rows
+        share = pl.multiple_of(flip(col % 2, odd) * lows, 8)
+        for d in range(1, nrow):
+            to = (row + d) % nrow
+            copy = pltpu.make_async_remote_copy(
+                src_ref=partial.at[pl.ds(pl.multiple_of(to * low_rows + share, 8), lows)],
+                dst_ref=amp_in.at[d - 1, pl.ds(share, lows)],
+                send_sem=amp_send.at[odd, d - 1],
+                recv_sem=amp_recv.at[odd, d - 1],
+                device_id=(to, col),
+                device_id_type=MESH,
+            )
+            copy.start()
+            amp_copies.append(copy)
+
+    sum_half(0)
     forward(len(bits) - 1)
-    own.wait()
-
-    total = jnp.zeros((ncol * pair_rows, 2 * uppers), f32)
-    for half in range(2):
-        total = total + lax.dot_general(
-            gathered[half],
-            weighted[:, pl.ds(half * piece, piece)],
-            (((1,), (1,)), ((), ())),
-            preferred_element_type=f32,
-        )
-    for mask in range(ncol):
-        base = mask * pair_rows
-        rows = total[base : base + lows, :uppers] + total[base + lows : base + 2 * lows, uppers:]
-        partial[pl.ds(pl.multiple_of(flip(col, mask) * lows, 8), lows), :] = rows
-
-    def amp_rows(owner):
-        return partial.at[pl.ds(pl.multiple_of(owner * low_rows, 8), low_rows)]
-
-    amp_copies = []
-    for d in range(1, nrow):
-        to = (row + d) % nrow
-        copy = pltpu.make_async_remote_copy(
-            src_ref=amp_rows(to),
-            dst_ref=amp_in.at[d - 1],
-            send_sem=amp_send.at[d - 1],
-            recv_sem=amp_recv.at[d - 1],
-            device_id=(to, col),
-            device_id_type=MESH,
-        )
-        copy.start()
-        amp_copies.append(copy)
+    sum_half(1)
     population = column_of(population_ref[...])
     lower_sym = lower_sym_ref[...]
     allowed = jnp.zeros(lower_sym.shape, jnp.int32)
@@ -316,11 +328,14 @@
     allowed = column_of(allowed)
     keep = jnp.where(upper_sym_ref[...] == allowed, 1.0, 0.0)
     amplitudes = partial[pl.ds(pl.multiple_of(row * low_rows, 8), low_rows), :]
+    for copy in amp_copies:
+        copy.wait_recv()
     for d in range(1, nrow):
-        amp_copies[d - 1].wait_recv()
         amplitudes = amplitudes + amp_in[d - 1]
     amp_ref[...] = amplitudes
     coef[5] = population * amplitudes * amplitudes * keep
+
+    first_tile = ((row + 1) % nrow) * chunk
 
     def scale_row(r, before):
         inside = place[1, pl.ds(r, 1), :]
@@ -332,7 +347,7 @@
         lane = pl.ds(pl.multiple_of(r * lines, lines), lines)
         windows[pl.ds(0, LANE), lane] = head.astype(bf16)
         windows[pl.ds(LANE, LANE), lane] = tail.astype(bf16)
-        return before + jnp.where(tile < 0, tail, 0.0)
+        return before + jnp.where(tile == first_tile - 1, tail, 0.0)
 
     before = lax.fori_loop(0, low_rows, scale_row, jnp.zeros((LANE, lines), f32))
     before = jnp.sum(before, axis=1, keepdims=True)
@@ -351,7 +366,8 @@
             device_id_type=MESH,
         )
 
-    def bin_chunk(m, carry):
+    def bin_chunk(i, carry):
+        m = (row + 1 + i) % nrow
         if not early:
             build(m, 0)
         slot = m if early else 0
@@ -368,20 +384,19 @@
 
     lax.fori_loop(0, nrow, bin_chunk, carry)
 
-    def add_chunk(m, _):
+    def add_chunk(m):
         value = outgoing[m, col].astype(f32)
         for d in range(1, ncol):
             col_copy(d, m).wait_recv()
             value = value + incoming[m, d - 1].astype(f32)
-        totals[m] = value
-        return 0
-
-    lax.fori_loop(0, nrow, add_chunk, 0)
+        return value
+
     row_copies = []
     for d in range(1, nrow):
         to = (row + d) % nrow
+        totals[d - 1] = add_chunk(to)
         copy = pltpu.make_async_remote_copy(
-            src_ref=totals.at[to],
+            src_ref=totals.at[d - 1],
             dst_ref=arrived.at[d - 1],
             send_sem=row_send.at[d - 1],
             recv_sem=row_recv.at[d - 1],
@@ -390,7 +405,7 @@
         )
         copy.start()
         row_copies.append(copy)
-    value = totals[row]
+    value = add_chunk(row)
     for d in range(1, nrow):
         row_copies[d - 1].wait_recv()
         value = value + arrived[d - 1]
@@ -430,8 +445,8 @@
     uppers = upper_vectors.shape[0]
     low_rows, lines = line_bin.shape
     quarter = basis // 4
-    pieces = lower_vectors.reshape(lows, 2, 2, quarter).transpose(2, 1, 0, 3)
-    pieces = pieces.reshape(2, 2 * lows, quarter)
+    cuts = [lower_vectors[:, i * quarter : (i + 1) * quarter] for i in (0, 2, 1, 3)]
+    pieces = jnp.concatenate(cuts, axis=0).reshape(2, 2 * lows, quarter)
     chunk = ncol * TILES_DEV
     count = low_rows * lines
     early = nrow * chunk * count * 2 <= 26 * 2**20
@@ -460,15 +475,15 @@
             pltpu.VMEM((nrow if early else 1, chunk, count), bf16),
             pltpu.VMEM((nrow, ncol, TILES_DEV, LANE), bf16),
             pltpu.VMEM((nrow, ncol - 1, TILES_DEV, LANE), bf16),
-            pltpu.VMEM((nrow, TILES_DEV, LANE), f32),
+            pltpu.VMEM((nrow - 1, TILES_DEV, LANE), f32),
             pltpu.VMEM((nrow - 1, TILES_DEV, LANE), f32),
             dma((2,)),
             dma((2,)),
             dma((2,)),
             dma((2, ncol)),
             dma((2, ncol)),
-            dma((nrow - 1,)),
-            dma((nrow - 1,)),
+            dma((2, nrow - 1)),
+            dma((2, nrow - 1)),
             dma((nrow, ncol - 1)),
             dma((nrow, ncol - 1)),
             dma((nrow - 1,)),

time: 69.7 us -> 63.5 us (0.911)
  Pallas kernels: 62.2 us -> 57.7 us
  local copies, waits for them, and re-layouts: 6.6 us -> 3.99 us
  other arithmetic: 0 us -> 0.94 us
    pallas_call x1, Pallas kernels: 62.2 us -> 57.7 us  [shards(): pl.pallas_call(functools.partial(kernel, nrow, ncol), out_shape=(jax.Shap...]
    reshape x2 -> x0, local copies, waits for them, and re-layouts: 3.88 us -> none  [shards(): pieces = lower_vectors.reshape(lows, 2, 2, quarter).transpose(2, 1, 0, 3)]
    slice x0 -> x1, local copies, waits for them, and re-layouts: none -> 1.27 us  [shards(): lower_vectors[:, i * quarter:(i + 1) * quarter]]
    concatenate x0 -> x1, other arithmetic: none -> 0.94 us  [shards(): pieces = jnp.concatenate(cuts, axis=0).reshape(2, 2 * lows, quarter)]
where the time goes in v2:
time: 63.5 us; the launch traced here: 63.2 us
  Pallas kernels  57.7 us (91%)
  local copies, waits for them, and re-layouts  3.99 us (6%)
  other arithmetic  0.94 us (1%)
  between operations  0.64 us (1%)
    pallas_call x1, Pallas kernels, shards(): pl.pallas_call(functools.partial(kernel, nrow, ncol), out_shape=(jax.Shap...  57.7 us
    unnamed x2, local copies, waits for them, and re-layouts  2.72 us
    slice x1, local copies, waits for them, and re-layouts, shards(): lower_vectors[:, i * quarter:(i + 1) * quarter]  1.27 us

profile of v2, /device:TPU:0, one launch (start us, length us, event | category | flops | bytes accessed | tf_op | source)
XLA Modules:
  0.0 63.2 jit_solution(7202429332626712035)
XLA Ops:
  0.6 1.3 %fusion = (bf16[24,4096]{1,0:T(8,128)(2,1)S(1)}, bf16[24,4096]{1,0:T(8,128)(2,1)S(1)}, bf16[24,4096]{1,0:T(8,128)(2,1)S(1)}, bf16[24,4096]{1,0:T(8,128)(2,1)S(1)}) fusion(bf16[24,16384]{1,0:T(8,128)(2,1)} %param.14), kind=kLoop, calls=%fused_computation.1 | loop fusion | bytes 1572864 | tf_op jit(solution)/shard_map/slice | solution.py:448
  1.9 0.9 %pad_maximum_fusion = bf16[96,4096]{1,0:T(8,128)(2,1)} fusion(bf16[24,4096]{1,0:T(8,128)(2,1)S(1)} %get-tuple-element.8, bf16[24,4096]{1,0:T(8,128)(2,1)S(1)} %get-tuple-element.9, bf16[24,4096]{1,0:T(8,128)(2,1)S(1)} %get-tuple-element.7, bf16[24,4096]{1,0:T(8,128)(2,1)S(1)} %get-tuple-element.6), kind=kLoop, calls=%fused_computation | loop fusion | flops 3145728 | bytes 1572864 | tf_op jit(solution)/shard_map/concatenate | solution.py:449
  2.8 57.7 %shard_map.149 = (f32[48,128]{1,0:T(8,128)}, f32[64,128]{1,0:T(8,128)}) custom-call(bf16[2,48,4096]{2,1,0:T(8,128)(2,1)} %bitcast.6, bf16[128,16384]{1,0:T(8,128)(2,1)} %upper_ref.1, bf16[3,256,256]{2,1,0:T(8,128)(2,1)} %vib_ref.1, f32[3,64]{1,0:T(4,128)} %rot_ref.1, f32[1,48]{1,0:T(1,128)} %bitcast.8, f32[1,48]{1,0:T(1,128)} %bitcast.9, s32[1,48]{1,0:T(1,128)} %bitcast.10, ...), custom_call_target="tpu_custom_call" | custom-call | tf_op jit(solution)/shard_map/pallas_call | solution.py:457
  60.5 1.3 %copy.18 = f32[48,128]{1,0:T(8,128)} copy(f32[48,128]{1,0:T(8,128)} %get-tuple-element.12) | data formatting | bytes 49152
  61.9 1.4 %copy.19 = f32[8192]{0:T(1024)} copy(f32[8192]{0:T(1024)} %bitcast.7) | data formatting | bytes 65536

commit v3 on v2

--- a/solution.py
+++ b/solution.py
@@ -14,6 +14,7 @@
 LANE = 128
 TILES_DEV = GRID_DEV // LANE
 GROUP = 4
+PIECES = 4
 MESH = pl.DeviceIdType.MESH
 
 doppler_base = 1.5
@@ -91,8 +92,9 @@
     col = lax.axis_index("col")
     uppers, basis = upper_ref.shape
     slabs = basis // NV
-    two, pair_rows, piece = lower_ref.shape
-    lows = pair_rows // 2
+    lows = lower_ref.shape[0]
+    pieces, _, piece = gathered.shape
+    pair_rows = 2 * lows
     low_rows, lines = bin_ref.shape
     tiles = nrow * ncol * TILES_DEV
     chunk = ncol * TILES_DEV
@@ -101,12 +103,11 @@
     while bit:
         bits.append(bit)
         bit //= 2
-    orders = [bits, [bits[1], bits[0]] + bits[2:]]
+    both = [bits, [bits[1], bits[0]] + bits[2:]]
+    orders = [both[k % 2] for k in range(pieces)]
 
     load = pltpu.make_async_copy(upper_ref, padded.at[:, pl.ds(NV, basis)], local_sem.at[0])
     load.start()
-    own = pltpu.make_async_copy(lower_ref, gathered.at[:, pl.ds(0, pair_rows)], local_sem.at[1])
-    own.start()
 
     barrier = pltpu.get_barrier_semaphore()
     for d in range(1, ncol):
@@ -117,6 +118,9 @@
         pl.semaphore_signal(
             barrier, inc=1, device_id=((row + d) % nrow, col), device_id_type=MESH
         )
+    for k in range(pieces):
+        sides = [lower_ref[:, pl.ds(i * (basis // 2) + k * piece, piece)] for i in range(2)]
+        gathered[k, pl.ds(0, pair_rows), :] = jnp.concatenate(sides, axis=0)
     pl.semaphore_wait(barrier, ncol + nrow - 2)
 
     def slot_rows(mask):
@@ -124,13 +128,9 @@
         return pl.ds(at * pair_rows, pair_rows)
 
     def piece_copy(half, mask, bit):
-        if mask == 0:
-            src = lower_ref.at[half]
-        else:
-            src = gathered.at[half, slot_rows(mask)]
         to = mask ^ bit
         return pltpu.make_async_remote_copy(
-            src_ref=src,
+            src_ref=gathered.at[half, slot_rows(mask)],
             dst_ref=gathered.at[half, slot_rows(to)],
             send_sem=gather_send.at[half, to],
             recv_sem=gather_recv.at[half, to],
@@ -165,7 +165,7 @@
         started.append(copy)
 
     for level in range(len(bits)):
-        for half in range(2):
+        for half in range(pieces):
             send(half, 0, orders[half][level])
 
     broad = column_of(broadening_ref[...])
@@ -267,10 +267,10 @@
             masks = masks + [m ^ b for m in masks]
         return [(m, m ^ order[level]) for m in masks]
 
-    def forward(level, begin=0, end=None):
+    def forward(level, begin=0, end=None, halves=range(pieces)):
         count = len(slots_of(0, level))
         for i in range(begin, count if end is None else end):
-            for half in range(2):
+            for half in halves:
                 mask, slot = slots_of(half, level)[i]
                 piece_copy(half, mask, orders[half][level]).wait_recv()
                 for later in orders[half][level + 1 :]:
@@ -281,45 +281,42 @@
     pl.when(row < nrow - 1)(lambda: down.wait_recv())
 
     weigh_half(1)
-    forward(1, 1)
-    for level in range(2, len(bits) - 1):
-        forward(level)
-    own.wait()
-
-    side = ncol // 2 * pair_rows
-    amp_copies = []
-
-    def sum_half(odd):
-        total = jnp.zeros((side, 2 * uppers), f32)
-        for half in range(2):
+
+    last = len(bits) - 1
+    total = jnp.zeros((ncol * pair_rows, 2 * uppers), f32)
+    for step in range(pieces + 2):
+        if step < pieces:
+            if last > 1:
+                forward(1, 1, None, [step])
+            for level in range(2, last):
+                forward(level, 0, None, [step])
+        if step >= 2:
+            k = step - 2
+            forward(last, 0 if last > 1 else 1, None, [k])
             total = total + lax.dot_general(
-                gathered[half, pl.ds(odd * side, side)],
-                weighted[:, pl.ds(half * piece, piece)],
+                gathered[k],
+                weighted[:, pl.ds(k * piece, piece)],
                 (((1,), (1,)), ((), ())),
                 preferred_element_type=f32,
             )
-        for i in range(ncol // 2):
-            base = i * pair_rows
-            rows = total[base : base + lows, :uppers] + total[base + lows : base + 2 * lows, uppers:]
-            source = flip(col, 2 * i + odd)
-            partial[pl.ds(pl.multiple_of(source * lows, 8), lows), :] = rows
-        share = pl.multiple_of(flip(col % 2, odd) * lows, 8)
-        for d in range(1, nrow):
-            to = (row + d) % nrow
-            copy = pltpu.make_async_remote_copy(
-                src_ref=partial.at[pl.ds(pl.multiple_of(to * low_rows + share, 8), lows)],
-                dst_ref=amp_in.at[d - 1, pl.ds(share, lows)],
-                send_sem=amp_send.at[odd, d - 1],
-                recv_sem=amp_recv.at[odd, d - 1],
-                device_id=(to, col),
-                device_id_type=MESH,
-            )
-            copy.start()
-            amp_copies.append(copy)
-
-    sum_half(0)
-    forward(len(bits) - 1)
-    sum_half(1)
+    for i in range(ncol):
+        base = i * pair_rows
+        rows = total[base : base + lows, :uppers] + total[base + lows : base + 2 * lows, uppers:]
+        source = flip(col, 2 * (i % (ncol // 2)) + i // (ncol // 2))
+        partial[pl.ds(pl.multiple_of(source * lows, 8), lows), :] = rows
+    amp_copies = []
+    for d in range(1, nrow):
+        to = (row + d) % nrow
+        copy = pltpu.make_async_remote_copy(
+            src_ref=partial.at[pl.ds(pl.multiple_of(to * low_rows, 8), low_rows)],
+            dst_ref=amp_in.at[d - 1],
+            send_sem=amp_send.at[d - 1],
+            recv_sem=amp_recv.at[d - 1],
+            device_id=(to, col),
+            device_id_type=MESH,
+        )
+        copy.start()
+        amp_copies.append(copy)
     population = column_of(population_ref[...])
     lower_sym = lower_sym_ref[...]
     allowed = jnp.zeros(lower_sym.shape, jnp.int32)
@@ -422,6 +419,11 @@
     lax.fori_loop(0, nrow, drain, 0)
     pl.when(row < nrow - 1)(lambda: up.wait_send())
     pl.when(row > 0)(lambda: down.wait_send())
+
+
+def hand_over(amp_ref, spec_ref, amp_out, spec_out):
+    amp_out[...] = amp_ref[...]
+    spec_out[...] = spec_ref[...]
 
 
 def shards(
@@ -444,9 +446,7 @@
     lows, basis = lower_vectors.shape
     uppers = upper_vectors.shape[0]
     low_rows, lines = line_bin.shape
-    quarter = basis // 4
-    cuts = [lower_vectors[:, i * quarter : (i + 1) * quarter] for i in (0, 2, 1, 3)]
-    pieces = jnp.concatenate(cuts, axis=0).reshape(2, 2 * lows, quarter)
+    piece = basis // 2 // PIECES
     chunk = ncol * TILES_DEV
     count = low_rows * lines
     early = nrow * chunk * count * 2 <= 26 * 2**20
@@ -460,12 +460,12 @@
             jax.ShapeDtypeStruct((low_rows, lines), f32),
             jax.ShapeDtypeStruct((TILES_DEV, LANE), f32),
         ),
-        in_specs=[hbm, hbm, vmem, smem, vmem, vmem, vmem, vmem, smem, vmem, smem, vmem, vmem, vmem],
+        in_specs=[vmem, hbm, vmem, smem, vmem, vmem, vmem, vmem, smem, vmem, smem, vmem, vmem, vmem],
         out_specs=(vmem, vmem),
         scratch_shapes=[
             pltpu.VMEM((uppers, basis + 2 * NV), bf16),
             pltpu.VMEM((2 * uppers, basis // 2), bf16),
-            pltpu.VMEM((2, ncol * 2 * lows, quarter), bf16),
+            pltpu.VMEM((PIECES, ncol * 2 * lows, piece), bf16),
             pltpu.VMEM((ncol * lows, uppers), f32),
             pltpu.VMEM((nrow - 1, low_rows, lines), f32),
             pltpu.VMEM((6, low_rows, lines), f32),
@@ -477,13 +477,13 @@
             pltpu.VMEM((nrow, ncol - 1, TILES_DEV, LANE), bf16),
             pltpu.VMEM((nrow - 1, TILES_DEV, LANE), f32),
             pltpu.VMEM((nrow - 1, TILES_DEV, LANE), f32),
+            dma((1,)),
             dma((2,)),
             dma((2,)),
-            dma((2,)),
-            dma((2, ncol)),
-            dma((2, ncol)),
-            dma((2, nrow - 1)),
-            dma((2, nrow - 1)),
+            dma((PIECES, ncol)),
+            dma((PIECES, ncol)),
+            dma((nrow - 1,)),
+            dma((nrow - 1,)),
             dma((nrow, ncol - 1)),
             dma((nrow, ncol - 1)),
             dma((nrow - 1,)),
@@ -493,7 +493,7 @@
             collective_id=0, has_side_effects=True, vmem_limit_bytes=58 * 2**20
         ),
     )(
-        pieces,
+        lower_vectors,
         upper_vectors,
         vib_dipole,
         rot_factor,
@@ -508,6 +508,15 @@
         line_bin,
         bin_offset,
     )
+    amplitudes, spectrum = pl.pallas_call(
+        hand_over,
+        out_shape=(
+            jax.ShapeDtypeStruct((low_rows, lines), f32),
+            jax.ShapeDtypeStruct((TILES_DEV, LANE), f32),
+        ),
+        in_specs=[vmem, vmem],
+        out_specs=(vmem, vmem),
+    )(amplitudes, spectrum)
     return (amplitudes, spectrum.reshape(GRID_DEV))
 
 

time: 63.5 us -> 59.5 us (0.937)
  local copies, waits for them, and re-layouts: 3.99 us -> 0 us
  other arithmetic: 0.94 us -> 0 us
  Pallas kernels: 57.7 us -> 58.6 us
    unnamed x2 -> x0, local copies, waits for them, and re-layouts: 2.72 us -> none
    pallas_call x0 -> x1, Pallas kernels: none -> 1.4 us  [shards(): pl.pallas_call(hand_over, out_shape=(jax.ShapeDtypeStruct((low_rows, line...]
    slice x1 -> x0, local copies, waits for them, and re-layouts: 1.27 us -> none  [shards(): lower_vectors[:, i * quarter:(i + 1) * quarter]]
    concatenate x1 -> x0, other arithmetic: 0.94 us -> none  [shards(): pieces = jnp.concatenate(cuts, axis=0).reshape(2, 2 * lows, quarter)]
where the time goes in v3:
time: 59.5 us; the launch traced here: 59.3 us
  Pallas kernels  58.6 us (98%)
  between operations  0.64 us (1%)
    pallas_call x1, Pallas kernels, shards(): pl.pallas_call(functools.partial(kernel, nrow, ncol), out_shape=(jax.Shap...  57.2 us
    pallas_call x1, Pallas kernels, shards(): pl.pallas_call(hand_over, out_shape=(jax.ShapeDtypeStruct((low_rows, line...  1.4 us

profile of v3, /device:TPU:0, one launch (start us, length us, event | category | flops | bytes accessed | tf_op | source)
XLA Modules:
  0.0 59.3 jit_solution(4174765879621061672)
XLA Ops:
  0.6 57.2 %shard_map.149 = (f32[48,128]{1,0:T(8,128)}, f32[64,128]{1,0:T(8,128)}) custom-call(bf16[24,16384]{1,0:T(8,128)(2,1)} %lower_ref.1, bf16[128,16384]{1,0:T(8,128)(2,1)} %upper_ref.1, bf16[3,256,256]{2,1,0:T(8,128)(2,1)} %vib_ref.1, f32[3,64]{1,0:T(4,128)} %rot_ref.1, f32[1,48]{1,0:T(1,128)} %bitcast.5, f32[1,48]{1,0:T(1,128)} %bitcast.6, s32[1,48]{1,0:T(1,128)} %bitcast.7, ...), custom_call_target="tpu_custom_call" | custom-call | tf_op jit(solution)/shard_map/pallas_call | solution.py:457
  57.9 1.4 %shard_map.150 = (f32[48,128]{1,0:T(8,128)}, f32[64,128]{1,0:T(8,128)}) custom-call(f32[48,128]{1,0:T(8,128)} %get-tuple-element.6.amp_ref, f32[64,128]{1,0:T(8,128)} %get-tuple-element.7.spec_ref), custom_call_target="tpu_custom_call" | custom-call | tf_op jit(solution)/shard_map/pallas_call | solution.py:511
